TPU v7x, 256 devices: a whole 4x4x8 slice. The times are simulated.
256 devices in a mesh: ctx: 16 (over y, x_hi, core), head: 16 (over x_lo, z).
Axes of the slice: x: 4 (x_hi: 2, x_lo: 2; x = x_hi * 2 + x_lo), y: 4, z: 8, core: 2. Of those that a mesh axis runs over, the one named last changes fastest.
Arguments:
- tokens: bfloat16 [16384, 2048], P('ctx', 'head'), may hold values from -6 to 6
- w_query: bfloat16 [2048, 2048], P(None, 'head'), may hold values from -0.125 to 0.125
- w_value: bfloat16 [2048, 2048], P(None, 'head'), may hold values from -0.125 to 0.125
- w_out: bfloat16 [2048, 2048], P('head'), may hold values from -1.5 to 1.5
- doc_lengths: int32 [2], replicated, may hold values from 1024 to 8192, as said below
Outputs:
- layer_out: bfloat16 [16384, 2048], P('ctx', 'head')
Inputs may be any that keep to these rules, and one draw needn't show every extreme that they name: `doc_lengths`: one of the two documents, drawn from the seed, has the full length 8192; the other has at least 1024 valid tokens.
All inputs are finite; a program needn't handle non-finite values.
Results may differ from a plain program's by a relative error of at most 0.02.
Values may be sent and summed in bfloat16 or wider, within the bound.
No kernel may reach another device: no remote copies, remote signals or barrier semaphores. Data moves between devices by JAX's collectives and lax.ppermute only.
A program may use at most 64 MiB of HBM per device.

v0:
```python
import itertools
import math

import jax
import jax.numpy as jnp
from jax import lax
from jax.experimental import pallas as pl
from jax.experimental.pallas import tpu as pltpu
from jax.sharding import Mesh
from jax.sharding import PartitionSpec as P

HD = 128
ROWS = 1024
HEAD = ("xl", "z")
CTX = ("yh", "yl", "xh", "core")
AXES = CTX + HEAD
SCORE_BOUND = 24.0
SCALE = SCORE_BOUND * math.log2(math.e)
VMEM = pl.BlockSpec(memory_space=pltpu.VMEM)
SMEM = pl.BlockSpec(memory_space=pltpu.SMEM)
F32 = jnp.float32
BF16 = jnp.bfloat16


def hop(value, axes, target):
    places = list(itertools.product(*(range(lax.axis_size(a)) for a in axes)))
    number = {place: i for i, place in enumerate(places)}
    return lax.ppermute(value, axes, [(number[c], number[tuple(target(*c))]) for c in places])


def swap(value, *axes):
    return hop(value, axes, lambda *c: tuple(1 - i for i in c))


def z_step(value, way):
    depth = lax.axis_size("z")
    return hop(value, ("z",), lambda z: ((z - way) % depth,))


def params(mib):
    return pltpu.CompilerParams(vmem_limit_bytes=mib * 2**20)


def call(kernel, outs, smem_count, args, name, flops, limit=24):
    moved = sum(math.prod(a.shape) * a.dtype.itemsize for a in [*args, *outs])
    return pl.pallas_call(
        kernel,
        out_shape=outs,
        in_specs=[SMEM] * smem_count + [VMEM] * (len(args) - smem_count),
        out_specs=[VMEM] * len(outs),
        compiler_params=params(limit),
        cost_estimate=pl.CostEstimate(flops=flops, bytes_accessed=moved, transcendentals=0),
        name=name,
    )(*args)


def after(value, *others):
    return lax.optimization_barrier((value, *others))[0]


def valid_rows(doc_ref, mask):
    in_doc = (lax.axis_index("yl") * 2 + lax.axis_index("xh")) * 2 + lax.axis_index("core")
    return doc_ref[lax.axis_index("yh")] - (in_doc ^ mask) * ROWS


def contract(weights, jobs, name, finish=None, outs=None, smem=()):
    width = sum(w.shape[1] for w in weights)
    flat, plan = [], []
    for total, *terms in jobs:
        plan.append((total is not None, [t[0] for t in terms]))
        flat += ([total] if total is not None else []) + [b for t in terms for b in t[1:]]
    rows = jobs[0][1][1].shape[0]
    tile = 256
    if outs is None:
        outs = [jax.ShapeDtypeStruct((rows, width), F32)] * len(jobs)
    n_s, n_w, n_f = len(smem), len(weights), len(flat)
    depth = lax.axis_size("z")

    def kernel(*refs):
        w_refs = refs[n_s : n_s + n_w]
        b_refs = list(refs[n_s + n_w : n_s + n_w + n_f])
        o_refs = refs[n_s + n_w + n_f :]
        xl, z = lax.axis_index("xl"), lax.axis_index("z")
        taken = {}

        def weight(step):
            if step not in taken:
                z_at = (z + depth + step) % depth
                halves = []
                for side in (xl, 1 - xl):
                    first = pl.multiple_of((side * depth + z_at) * HD, HD)
                    rows_here = [w[pl.ds(first, HD), :] for w in w_refs]
                    halves.append(jnp.concatenate(rows_here, axis=1))
                taken[step] = jnp.concatenate(halves, axis=0)
            return taken[step]

        for index, (has_total, steps) in enumerate(plan):
            total_ref = b_refs.pop(0) if has_total else None
            pairs = [(s, b_refs.pop(0), b_refs.pop(0)) for s in steps]
            for first in range(0, rows, tile):
                here = slice(first, first + tile)
                total = None if total_ref is None else total_ref[here, :]
                for s, one, two in pairs:
                    both = jnp.concatenate([one[here, :], two[here, :]], axis=1)
                    term = jnp.dot(both, weight(s), preferred_element_type=F32)
                    total = term if total is None else total + term
                if finish is None:
                    o_refs[index][here, :] = total.astype(o_refs[index].dtype)
                else:
                    finish(refs[:n_s], o_refs, total, first, tile)

    terms = sum(len(steps) for _, steps in plan)
    return call(
        kernel,
        outs,
        n_s,
        [*smem, *weights, *flat],
        name,
        2 * rows * 256 * width * terms,
    )


def finish_units(smem, outs, total, first, tile):
    here = slice(first, first + tile)
    row = lax.broadcasted_iota(jnp.int32, (tile, HD), 0) + first + lax.axis_index("xl") * (ROWS // 2)
    valid = row < valid_rows(smem[0], 0)
    for out, start in zip(outs, (0, 2 * HD)):
        proj = total[:, start : start + HD]
        unit = proj * lax.rsqrt(jnp.sum(proj * proj, axis=-1, keepdims=True) + 1e-06)
        value = jnp.where(valid, total[:, start + HD : start + 2 * HD], 0.0)
        out[here, :HD] = unit.astype(BF16)
        out[here, HD:] = value.astype(BF16)


def finish_out(smem, outs, total, first, tile):
    here = slice(first, first + tile)
    outs[0][here, :] = total[:, :HD].astype(BF16)
    outs[1][here, :] = total[:, HD:].astype(BF16)


def split_rows(block, name):
    half = block.shape[0] // 2

    def kernel(b_ref, mine_ref, theirs_ref):
        side = lax.axis_index("xl")
        mine_ref[...] = b_ref[pl.ds(pl.multiple_of(side * half, half), half), :]
        theirs_ref[...] = b_ref[pl.ds(pl.multiple_of((1 - side) * half, half), half), :]

    out = jax.ShapeDtypeStruct((half, block.shape[1]), block.dtype)
    return call(kernel, [out, out], 0, [block], name, 0)


def join_rows(mine, theirs, name, lead=False):
    half, width = mine.shape

    def kernel(m_ref, t_ref, o_ref, *lead_ref):
        side = lax.axis_index("xl")
        for ref, at in ((m_ref, side), (t_ref, 1 - side)):
            here = pl.ds(pl.multiple_of(at * half, half), half)
            o_ref[here, :] = ref[...]
            for l_ref in lead_ref:
                l_ref[here, :] = ref[:, :HD]

    outs = [jax.ShapeDtypeStruct((2 * half, width), mine.dtype)]
    if lead:
        outs.append(jax.ShapeDtypeStruct((2 * half, HD), mine.dtype))
    return call(kernel, outs, 0, [mine, theirs], name, 0)


def attend(doc_lengths, groups, blocks, name, out_type=F32, tile_q=512, tile_k=512):
    masks, blocks = zip(*blocks)
    n_b = len(blocks)
    flat, plan = [], []
    for queries, total, own in groups:
        plan.append((total is not None, own))
        flat += [queries] + ([total] if total is not None else [])
    rows = groups[0][0].shape[0]
    outs = [jax.ShapeDtypeStruct((rows, 2 * HD), out_type)] * len(groups)

    def kernel(*refs):
        limit = [valid_rows(refs[0], mask) for mask in masks]
        kv_refs = refs[1 : 1 + n_b]
        g_refs = list(refs[1 + n_b : 1 + n_b + len(flat)])
        o_refs = refs[1 + n_b + len(flat) :]
        for index, (has_total, own) in enumerate(plan):
            q_ref = g_refs.pop(0)
            t_ref = g_refs.pop(0) if has_total else None

            @pl.loop(0, rows // tile_q)
            def _(step):
                first = pl.multiple_of(step * tile_q, tile_q)
                here = pl.ds(first, tile_q)
                queries = q_ref[here, :]
                total = None if t_ref is None else t_ref[here, :]
                for b, kv in enumerate(kv_refs):
                    for start in range(0, kv.shape[0], tile_k):
                        keys = kv[start : start + tile_k, :HD]
                        values = kv[start : start + tile_k, HD:]
                        row = lax.broadcasted_iota(jnp.int32, (tile_k, HD), 0) + start
                        counted = jnp.where(row < limit[b], 1.0, 0.0).astype(BF16)
                        scores = lax.dot_general(
                            queries, keys, (((1,), (1,)), ((), ())), preferred_element_type=F32
                        )
                        weights = jnp.exp2(scores * SCALE - SCALE)
                        if own and b == 0:
                            q_at = lax.broadcasted_iota(jnp.int32, weights.shape, 0) + first
                            k_at = lax.broadcasted_iota(jnp.int32, weights.shape, 1) + start
                            weights = jnp.where(q_at == k_at, 0.0, weights)
                        term = jnp.dot(
                            weights.astype(BF16),
                            jnp.concatenate([values, counted], axis=1),
                            preferred_element_type=F32,
                        )
                        total = term if total is None else total + term
                o_refs[index][here, :] = total.astype(out_type)

    flops = len(groups) * n_b * 4 * rows * blocks[0].shape[0] * HD * 2
    return call(kernel, outs, 1, [doc_lengths, *blocks, *flat], name, flops)


def combine(doc_lengths, mine, theirs, name):
    rows = mine.shape[0]

    def kernel(doc_ref, a_ref, b_ref, o_ref):
        total = a_ref[...] + b_ref[...].astype(F32)
        row = lax.broadcasted_iota(jnp.int32, (rows, HD), 0)
        valid = row < valid_rows(doc_ref, 0)
        denom = jnp.where(valid, total[:, HD:], 1.0)
        o_ref[...] = jnp.where(valid, total[:, :HD] / denom, 0.0).astype(BF16)

    out = jax.ShapeDtypeStruct((rows, HD), BF16)
    return call(kernel, [out], 1, [doc_lengths, mine, theirs], name, rows * HD * 8)[0]


def column_parts(matrix, count):
    rows, width = matrix.shape[0], matrix.shape[1] // count

    def kernel(m_ref, o_ref):
        for i in range(count):
            o_ref[i] = m_ref[:, i * width : (i + 1) * width]

    out = jax.ShapeDtypeStruct((count, rows, width), matrix.dtype)
    return call(kernel, [out], 0, [matrix], "column_parts", 0)[0]


def gathered_product(block, weights, more, finish, outs, smem, name):
    assert lax.axis_size("z") == 8
    mine, theirs = split_rows(block, f"{name}_split")
    own, cross = {0: mine}, {0: swap(theirs, "xl")}
    for s in (1, 2, 3):
        for way in (-1, 1):
            own[way * s] = z_step(own[way * (s - 1)], way)
            held = cross[way * (s - 1)]
            cross[way * s] = z_step(after(held, own[way]) if s == 1 else held, way)
    own[4], cross[4] = z_step(own[-3], -1), z_step(cross[3], 1)
    weights = [*weights, *more((cross[0],))]

    def terms(*places):
        return [(d, own[d], cross[d]) for d in places]

    own[0] = after(own[0], own[3], own[-3])
    (total,) = contract(
        weights, [[None, *terms(0, 1, -1, 2, -2)]], f"{name}_near"
    )
    return contract(
        weights,
        [[total, *terms(3, -3, 4)]],
        f"{name}_far",
        finish=finish,
        outs=outs,
        smem=smem,
    )


def per_device(tokens, w_query, w_value, w_out, doc_lengths):
    rows = tokens.shape[0]
    heads = lax.axis_size(HEAD)

    half = rows // 2

    def partner_weights(early):
        return swap(after(w_query, *early), "xl"), swap(after(w_value, *early), "xl")

    mine, theirs = gathered_product(
        tokens,
        [w_query, w_value],
        partner_weights,
        finish_units,
        [jax.ShapeDtypeStruct((half, 2 * HD), BF16)] * 2,
        [doc_lengths],
        "project",
    )
    joined, unit = join_rows(mine, swap(theirs, "xl"), "join_units", lead=True)
    unit_other = swap(unit, "core")
    from_y, from_x = swap(joined, "yl"), swap(joined, "xh")
    from_yx = swap(joined, "yl", "xh")
    parts = column_parts(w_out, heads)

    own, other = attend(
        doc_lengths, [(unit, None, True), (unit_other, None, False)], [(0, joined)], "attend_own", tile_q=256
    )
    w_cols = lax.all_to_all(after(parts, own, from_y), HEAD, 0, 0).reshape(heads * HD, HD)
    own, other = attend(
        doc_lengths,
        [(unit, own, False), (unit_other, other, False)],
        [(4, from_y), (2, from_x)],
        "attend_near",
    )
    (other,) = attend(
        doc_lengths, [(unit_other, other, False)], [(6, from_yx)], "attend_far_other", out_type=BF16
    )
    theirs = swap(other, "core")
    (own,) = attend(doc_lengths, [(unit, own, False)], [(6, from_yx)], "attend_far_own")
    attended = combine(doc_lengths, after(own, w_cols), theirs, "combine")

    mine, theirs = gathered_product(
        attended,
        [w_cols],
        lambda early: [swap(after(w_cols, *early), "xl")],
        finish_out,
        [jax.ShapeDtypeStruct((half, HD), BF16)] * 2,
        [],
        "output",
    )
    return join_rows(mine, swap(theirs, "xl"), "join_out")[0]


def solution(mesh):
    finer = Mesh(mesh.devices.reshape(2, 2, 2, 2, 2, 8), AXES)
    return jax.shard_map(
        per_device,
        mesh=finer,
        in_specs=(P(CTX, HEAD), P(None, HEAD), P(None, HEAD), P(HEAD, None), P()),
        out_specs=P(CTX, HEAD),
        check_vma=False,
    )
```

profile of v0, /device:TPU:16, one launch (start us, length us, event | category | flops | bytes accessed | tf_op | source)
XLA Modules:
  0.0 129.1 jit_solution(15736179200477357102)
XLA Ops:
  2.6 1.9 %collective-permute-start.6 = (bf16[512,128]{1,0:T(8,128)(2,1)S(1)}, bf16[512,128]{1,0:T(8,128)(2,1)S(1)}, u32[]{:S(2)}, u32[]{:S(2)}) collective-permute-start(bf16[512,128]{1,0:T(8,128)(2,1)S(1)} %get-tuple-element.34.refs_4_), channel_id=1, source_target_pairs={{0,1},{1,2},{2,3},{3,4},{4,5},{5,6},{6,7},{7,0},{8,9},{9,10},{10,1... | collective-permute-start | bytes 393224 | tf_op jit(solution)/shard_map/ppermute | solution.py:28
  4.5 3.9 %collective-permute-start.3 = (bf16[512,128]{1,0:T(8,128)(2,1)S(1)}, bf16[512,128]{1,0:T(8,128)(2,1)S(1)}, u32[]{:S(2)}, u32[]{:S(2)}) collective-permute-start(bf16[512,128]{1,0:T(8,128)(2,1)S(1)} %get-tuple-element.34.refs_4_), channel_id=1, source_target_pairs={{0,7},{1,0},{2,1},{3,2},{4,3},{5,4},{6,5},{7,6},{8,15},{9,8},{10,9... | collective-permute-start | bytes 393224 | tf_op jit(solution)/shard_map/ppermute | solution.py:28
  11.6 3.2 %collective-permute-start.4 = (bf16[512,128]{1,0:T(8,128)(2,1)S(1)}, bf16[512,128]{1,0:T(8,128)(2,1)S(1)}, u32[]{:S(2)}, u32[]{:S(2)}) collective-permute-start(bf16[512,128]{1,0:T(8,128)(2,1)S(1)} %collective-permute-done.3.refs_6_), channel_id=1, source_target_pairs={{0,7},{1,0},{2,1},{3,2},{4,3},{5,4},{6,5},{7,6},{8,15},{9,8},{10,9... | collective-permute-start | bytes 393224 | tf_op jit(solution)/shard_map/ppermute | solution.py:28
  17.9 2.0 %collective-permute-done.9.refs_7_ = bf16[512,128]{1,0:T(8,128)(2,1)S(1)} collective-permute-done((bf16[512,128]{1,0:T(8,128)(2,1)S(1)}, bf16[512,128]{1,0:T(8,128)(2,1)S(1)}, u32[]{:S(2)}, u32[]{:S(2)}) %collective-permute-start.9) | collective-permute-done | bytes 131104 | tf_op jit(solution)/shard_map/ppermute | solution.py:28
  19.8 3.1 %collective-permute-start.11 = (bf16[512,128]{1,0:T(8,128)(2,1)S(1)}, bf16[512,128]{1,0:T(8,128)(2,1)S(1)}, u32[]{:S(2)}, u32[]{:S(2)}) collective-permute-start(bf16[512,128]{1,0:T(8,128)(2,1)S(1)} %collective-permute-done.9.refs_7_), channel_id=1, source_target_pairs={{0,7},{1,0},{2,1},{3,2},{4,3},{5,4},{6,5},{7,6},{8,15},{9,8},{10,9... | collective-permute-start | bytes 393224 | tf_op jit(solution)/shard_map/ppermute | solution.py:28
  24.0 2.3 %collective-permute-done.8.refs_8_ = bf16[512,128]{1,0:T(8,128)(2,1)S(1)} collective-permute-done((bf16[512,128]{1,0:T(8,128)(2,1)S(1)}, bf16[512,128]{1,0:T(8,128)(2,1)S(1)}, u32[]{:S(2)}, u32[]{:S(2)}) %collective-permute-start.8) | collective-permute-done | bytes 131104 | tf_op jit(solution)/shard_map/ppermute | solution.py:28
  27.2 3.3 %collective-permute-start.13 = (bf16[512,128]{1,0:T(8,128)(2,1)S(1)}, bf16[512,128]{1,0:T(8,128)(2,1)S(1)}, u32[]{:S(2)}, u32[]{:S(2)}) collective-permute-start(bf16[512,128]{1,0:T(8,128)(2,1)S(1)} %collective-permute-done.11.refs_11_), channel_id=1, source_target_pairs={{0,7},{1,0},{2,1},{3,2},{4,3},{5,4},{6,5},{7,6},{8,15},{9,8},{10,9... | collective-permute-start | bytes 393224 | tf_op jit(solution)/shard_map/ppermute | solution.py:28
  31.8 2.6 %collective-permute-done.13.refs_7_ = bf16[512,128]{1,0:T(8,128)(2,1)S(1)} collective-permute-done((bf16[512,128]{1,0:T(8,128)(2,1)S(1)}, bf16[512,128]{1,0:T(8,128)(2,1)S(1)}, u32[]{:S(2)}, u32[]{:S(2)}) %collective-permute-start.13) | collective-permute-done | bytes 131104 | tf_op jit(solution)/shard_map/ppermute | solution.py:28
  34.4 3.7 %collective-permute-start.16 = (bf16[512,128]{1,0:T(8,128)(2,1)S(1)}, bf16[512,128]{1,0:T(8,128)(2,1)S(1)}, u32[]{:S(2)}, u32[]{:S(2)}) collective-permute-start(bf16[512,128]{1,0:T(8,128)(2,1)S(1)} %collective-permute-done.13.refs_7_), channel_id=1, source_target_pairs={{0,7},{1,0},{2,1},{3,2},{4,3},{5,4},{6,5},{7,6},{8,15},{9,8},{10,9... | collective-permute-start | bytes 393224 | tf_op jit(solution)/shard_map/ppermute | solution.py:28
  43.2 8.6 %collective-permute-done.17.t_ref = bf16[512,256]{1,0:T(8,128)(2,1)S(1)} collective-permute-done((bf16[512,256]{1,0:T(8,128)(2,1)S(1)}, bf16[512,256]{1,0:T(8,128)(2,1)S(1)}, u32[]{:S(2)}, u32[]{:S(2)}) %collective-permute-start.17) | collective-permute-done | bytes 262176 | tf_op jit(solution)/shard_map/ppermute | solution.py:28
  53.3 2.8 %collective-permute-start.21 = (bf16[1024,256]{1,0:T(8,128)(2,1)S(1)}, bf16[1024,256]{1,0:T(8,128)(2,1)S(1)}, u32[]{:S(2)}, u32[]{:S(2)}) collective-permute-start(bf16[1024,256]{1,0:T(8,128)(2,1)S(1)} %get-tuple-element.39.refs_1_), channel_id=1, source_target_pairs={{0,32},{32,0},{1,33},{33,1},{2,34},{34,2},{3,35},{35,3},{4,36},{36... | collective-permute-start | bytes 1572872 | tf_op jit(solution)/shard_map/ppermute | solution.py:28
  57.8 6.0 %attend_own.1 = (f32[1024,256]{1,0:T(8,128)S(1)}, f32[1024,256]{1,0:T(8,128)S(1)}) custom-call(s32[2]{0:T(128)S(1)} %copy-done.6, bf16[1024,256]{1,0:T(8,128)(2,1)S(1)} %get-tuple-element.39.refs_1_, bf16[1024,128]{1,0:T(8,128)(2,1)S(1)} %get-tuple-element.40.refs_2_.refs_3_, bf16[1024,128]{1,0:T(8,128)(2,1)S(1)} %collective-permute-done.18.refs_3_.refs_5_.refs_2_), custom_call_target="tpu_custom_call" | custom-call | flops 2147483648 | bytes 3145736 | tf_op jit(solution)/shard_map/attend_own/pallas_call | solution.py:46
  65.9 5.2 %all-to-all-start = ((bf16[16,128,128]{2,1,0:T(8,128)(2,1)}), bf16[16,128,128]{2,1,0:T(8,128)(2,1)S(1)}, u32[]{:S(2)}, u32[]{:S(2)}) async-start(bf16[16,128,128]{2,1,0:T(8,128)(2,1)} %column_parts.1), calls=%async_computation | async-start | bytes 1048576 | tf_op jit(solution)/shard_map/all_to_all | solution.py:302
  73.5 6.0 %attend_near.1 = (f32[1024,256]{1,0:T(8,128)S(1)}, f32[1024,256]{1,0:T(8,128)S(1)}) custom-call(s32[2]{0:T(128)S(1)} %copy-done.6, bf16[1024,256]{1,0:T(8,128)(2,1)S(1)} %collective-permute-done.19.refs_1_, bf16[1024,256]{1,0:T(8,128)(2,1)S(1)} %collective-permute-done.21.refs_2_, bf16[1024,128]{1,0:T(8,128)(2,1)S(1)} %get-tuple-element.40.refs_2_.refs_3_, ...), custom_call_target="tpu_custom_call" | custom-call | flops 4294967296 | bytes 5767176 | tf_op jit(solution)/shard_map/attend_near/pallas_call | solution.py:46
  80.6 2.2 %attend_far_other.1 = bf16[1024,256]{1,0:T(8,128)(2,1)S(1)} custom-call(s32[2]{0:T(128)S(1)} %copy-done.6, bf16[1024,256]{1,0:T(8,128)(2,1)S(1)} %collective-permute-done.20.refs_1_, bf16[1024,128]{1,0:T(8,128)(2,1)S(1)} %copy-done.8, f32[1024,256]{1,0:T(8,128)S(1)} %get-tuple-element.46.refs_3_), custom_call_target="tpu_custom_call" | custom-call | flops 1073741824 | bytes 2359304 | tf_op jit(solution)/shard_map/attend_far_other/pallas_call | solution.py:46
  82.9 2.2 %attend_far_own.1.a_ref = f32[1024,256]{1,0:T(8,128)S(1)} custom-call(s32[2]{0:T(128)S(1)} %copy-done.6, bf16[1024,256]{1,0:T(8,128)(2,1)S(1)} %collective-permute-done.20.refs_1_, bf16[1024,128]{1,0:T(8,128)(2,1)S(1)} %get-tuple-element.40.refs_2_.refs_3_, f32[1024,256]{1,0:T(8,128)S(1)} %get-tuple-element.44.refs_3_), custom_call_target="tpu_custom_call" | custom-call | flops 1073741824 | bytes 2883592 | tf_op jit(solution)/shard_map/attend_far_own/pallas_call | solution.py:46
  88.8 2.5 %collective-permute-start.25 = (bf16[512,128]{1,0:T(8,128)(2,1)S(1)}, bf16[512,128]{1,0:T(8,128)(2,1)S(1)}, u32[]{:S(2)}, u32[]{:S(2)}) collective-permute-start(bf16[512,128]{1,0:T(8,128)(2,1)S(1)} %get-tuple-element.50.refs_2_), channel_id=1, source_target_pairs={{0,7},{1,0},{2,1},{3,2},{4,3},{5,4},{6,5},{7,6},{8,15},{9,8},{10,9... | collective-permute-start | bytes 393224 | tf_op jit(solution)/shard_map/ppermute | solution.py:28
  93.8 2.1 %collective-permute-start.28 = (bf16[512,128]{1,0:T(8,128)(2,1)S(1)}, bf16[512,128]{1,0:T(8,128)(2,1)S(1)}, u32[]{:S(2)}, u32[]{:S(2)}) collective-permute-start(bf16[512,128]{1,0:T(8,128)(2,1)S(1)} %get-tuple-element.50.refs_2_), channel_id=1, source_target_pairs={{0,1},{1,2},{2,3},{3,4},{4,5},{5,6},{6,7},{7,0},{8,9},{9,10},{10,1... | collective-permute-start | bytes 393224 | tf_op jit(solution)/shard_map/ppermute | solution.py:28
  97.5 2.5 %collective-permute-done.28.refs_6_ = bf16[512,128]{1,0:T(8,128)(2,1)S(1)} collective-permute-done((bf16[512,128]{1,0:T(8,128)(2,1)S(1)}, bf16[512,128]{1,0:T(8,128)(2,1)S(1)}, u32[]{:S(2)}, u32[]{:S(2)}) %collective-permute-start.28) | collective-permute-done | bytes 131104 | tf_op jit(solution)/shard_map/ppermute | solution.py:28
  101.9 3.2 %collective-permute-start.33 = (bf16[512,128]{1,0:T(8,128)(2,1)S(1)}, bf16[512,128]{1,0:T(8,128)(2,1)S(1)}, u32[]{:S(2)}, u32[]{:S(2)}) collective-permute-start(bf16[512,128]{1,0:T(8,128)(2,1)S(1)} %collective-permute-done.31.refs_5_), channel_id=1, source_target_pairs={{0,7},{1,0},{2,1},{3,2},{4,3},{5,4},{6,5},{7,6},{8,15},{9,8},{10,9... | collective-permute-start | bytes 393224 | tf_op jit(solution)/shard_map/ppermute | solution.py:28
  110.7 2.0 %collective-permute-start.35 = (bf16[512,128]{1,0:T(8,128)(2,1)S(1)}, bf16[512,128]{1,0:T(8,128)(2,1)S(1)}, u32[]{:S(2)}, u32[]{:S(2)}) collective-permute-start(bf16[512,128]{1,0:T(8,128)(2,1)S(1)} %collective-permute-done.33.refs_9_), channel_id=1, source_target_pairs={{0,7},{1,0},{2,1},{3,2},{4,3},{5,4},{6,5},{7,6},{8,15},{9,8},{10,9... | collective-permute-start | bytes 393224 | tf_op jit(solution)/shard_map/ppermute | solution.py:28
  112.6 2.4 %collective-permute-start.27 = (bf16[512,128]{1,0:T(8,128)(2,1)S(1)}, bf16[512,128]{1,0:T(8,128)(2,1)S(1)}, u32[]{:S(2)}, u32[]{:S(2)}) collective-permute-start(bf16[512,128]{1,0:T(8,128)(2,1)S(1)} %collective-permute-done.26.refs_8_), channel_id=1, source_target_pairs={{0,7},{1,0},{2,1},{3,2},{4,3},{5,4},{6,5},{7,6},{8,15},{9,8},{10,9... | collective-permute-start | bytes 393224 | tf_op jit(solution)/shard_map/ppermute | solution.py:28
  117.1 2.9 %collective-permute-start.38 = (bf16[512,128]{1,0:T(8,128)(2,1)S(1)}, bf16[512,128]{1,0:T(8,128)(2,1)S(1)}, u32[]{:S(2)}, u32[]{:S(2)}) collective-permute-start(bf16[512,128]{1,0:T(8,128)(2,1)S(1)} %collective-permute-done.35.refs_4_), channel_id=1, source_target_pairs={{0,7},{1,0},{2,1},{3,2},{4,3},{5,4},{6,5},{7,6},{8,15},{9,8},{10,9... | collective-permute-start | bytes 393224 | tf_op jit(solution)/shard_map/ppermute | solution.py:28
  124.9 3.5 %collective-permute-done.39.t_ref = bf16[512,128]{1,0:T(8,128)(2,1)S(1)} collective-permute-done((bf16[512,128]{1,0:T(8,128)(2,1)S(1)}, bf16[512,128]{1,0:T(8,128)(2,1)S(1)}, u32[]{:S(2)}, u32[]{:S(2)}) %collective-permute-start.39) | collective-permute-done | bytes 131104 | tf_op jit(solution)/shard_map/ppermute | solution.py:28
  (98 shorter events, 48.8 us)
Async XLA Ops:
  1.0 7.4 %collective-permute-start = (bf16[512,128]{1,0:T(8,128)(2,1)S(1)}, bf16[512,128]{1,0:T(8,128)(2,1)S(1)}, u32[]{:S(2)}, u32[]{:S(2)}) collective-permute-start(bf16[512,128]{1,0:T(8,128)(2,1)S(1)} %get-tuple-element.30), channel_id=1, source_target_pairs={{0,8},{8,0},{1,9},{9,1},{2,10},{10,2},{3,11},{11,3},{4,12},{12,4},... | collective-permute-start | bytes 393224 | tf_op jit(solution)/shard_map/ppermute | solution.py:28
  2.6 9.1 %collective-permute-start.6 = (bf16[512,128]{1,0:T(8,128)(2,1)S(1)}, bf16[512,128]{1,0:T(8,128)(2,1)S(1)}, u32[]{:S(2)}, u32[]{:S(2)}) collective-permute-start(bf16[512,128]{1,0:T(8,128)(2,1)S(1)} %get-tuple-element.34.refs_4_), channel_id=1, source_target_pairs={{0,1},{1,2},{2,3},{3,4},{4,5},{5,6},{6,7},{7,0},{8,9},{9,10},{10,1... | collective-permute-start | bytes 393224 | tf_op jit(solution)/shard_map/ppermute | solution.py:28
  4.5 7.2 %collective-permute-start.3 = (bf16[512,128]{1,0:T(8,128)(2,1)S(1)}, bf16[512,128]{1,0:T(8,128)(2,1)S(1)}, u32[]{:S(2)}, u32[]{:S(2)}) collective-permute-start(bf16[512,128]{1,0:T(8,128)(2,1)S(1)} %get-tuple-element.34.refs_4_), channel_id=1, source_target_pairs={{0,7},{1,0},{2,1},{3,2},{4,3},{5,4},{6,5},{7,6},{8,15},{9,8},{10,9... | collective-permute-start | bytes 393224 | tf_op jit(solution)/shard_map/ppermute | solution.py:28
  8.4 29.6 %collective-permute-start.1 = (bf16[2048,128]{1,0:T(8,128)(2,1)}, bf16[2048,128]{1,0:T(8,128)(2,1)S(1)}, u32[]{:S(2)}, u32[]{:S(2)}) collective-permute-start(bf16[2048,128]{1,0:T(8,128)(2,1)} %refs_1_.3), channel_id=1, source_target_pairs={{0,8},{8,0},{1,9},{9,1},{2,10},{10,2},{3,11},{11,3},{4,12},{12,4},... | collective-permute-start | bytes 1572872 | tf_op jit(solution)/shard_map/ppermute | solution.py:28
  9.0 29.1 %collective-permute-start.2 = (bf16[2048,128]{1,0:T(8,128)(2,1)}, bf16[2048,128]{1,0:T(8,128)(2,1)S(1)}, u32[]{:S(2)}, u32[]{:S(2)}) collective-permute-start(bf16[2048,128]{1,0:T(8,128)(2,1)} %refs_2_.1), channel_id=1, source_target_pairs={{0,8},{8,0},{1,9},{9,1},{2,10},{10,2},{3,11},{11,3},{4,12},{12,4},... | collective-permute-start | bytes 1572872 | tf_op jit(solution)/shard_map/ppermute | solution.py:28
  17.9 8.4 %collective-permute-start.8 = (bf16[512,128]{1,0:T(8,128)(2,1)S(1)}, bf16[512,128]{1,0:T(8,128)(2,1)S(1)}, u32[]{:S(2)}, u32[]{:S(2)}) collective-permute-start(bf16[512,128]{1,0:T(8,128)(2,1)S(1)} %collective-permute-done.7.refs_12_), channel_id=1, source_target_pairs={{0,1},{1,2},{2,3},{3,4},{4,5},{5,6},{6,7},{7,0},{8,9},{9,10},{10,1... | collective-permute-start | bytes 393224 | tf_op jit(solution)/shard_map/ppermute | solution.py:28
  19.8 7.4 %collective-permute-start.11 = (bf16[512,128]{1,0:T(8,128)(2,1)S(1)}, bf16[512,128]{1,0:T(8,128)(2,1)S(1)}, u32[]{:S(2)}, u32[]{:S(2)}) collective-permute-start(bf16[512,128]{1,0:T(8,128)(2,1)S(1)} %collective-permute-done.9.refs_7_), channel_id=1, source_target_pairs={{0,7},{1,0},{2,1},{3,2},{4,3},{5,4},{6,5},{7,6},{8,15},{9,8},{10,9... | collective-permute-start | bytes 393224 | tf_op jit(solution)/shard_map/ppermute | solution.py:28
  27.2 7.2 %collective-permute-start.13 = (bf16[512,128]{1,0:T(8,128)(2,1)S(1)}, bf16[512,128]{1,0:T(8,128)(2,1)S(1)}, u32[]{:S(2)}, u32[]{:S(2)}) collective-permute-start(bf16[512,128]{1,0:T(8,128)(2,1)S(1)} %collective-permute-done.11.refs_11_), channel_id=1, source_target_pairs={{0,7},{1,0},{2,1},{3,2},{4,3},{5,4},{6,5},{7,6},{8,15},{9,8},{10,9... | collective-permute-start | bytes 393224 | tf_op jit(solution)/shard_map/ppermute | solution.py:28
  30.6 10.5 %collective-permute-start.14 = (bf16[512,128]{1,0:T(8,128)(2,1)S(1)}, bf16[512,128]{1,0:T(8,128)(2,1)S(1)}, u32[]{:S(2)}, u32[]{:S(2)}) collective-permute-start(bf16[512,128]{1,0:T(8,128)(2,1)S(1)} %collective-permute-done.12.refs_13_), channel_id=1, source_target_pairs={{0,1},{1,2},{2,3},{3,4},{4,5},{5,6},{6,7},{7,0},{8,9},{9,10},{10,1... | collective-permute-start | bytes 393224 | tf_op jit(solution)/shard_map/ppermute | solution.py:28
  31.8 9.2 %collective-permute-start.15 = (bf16[512,128]{1,0:T(8,128)(2,1)S(1)}, bf16[512,128]{1,0:T(8,128)(2,1)S(1)}, u32[]{:S(2)}, u32[]{:S(2)}) collective-permute-start(bf16[512,128]{1,0:T(8,128)(2,1)S(1)} %collective-permute-done.8.refs_8_), channel_id=1, source_target_pairs={{0,1},{1,2},{2,3},{3,4},{4,5},{5,6},{6,7},{7,0},{8,9},{9,10},{10,1... | collective-permute-start | bytes 393224 | tf_op jit(solution)/shard_map/ppermute | solution.py:28
  34.4 6.7 %collective-permute-start.16 = (bf16[512,128]{1,0:T(8,128)(2,1)S(1)}, bf16[512,128]{1,0:T(8,128)(2,1)S(1)}, u32[]{:S(2)}, u32[]{:S(2)}) collective-permute-start(bf16[512,128]{1,0:T(8,128)(2,1)S(1)} %collective-permute-done.13.refs_7_), channel_id=1, source_target_pairs={{0,7},{1,0},{2,1},{3,2},{4,3},{5,4},{6,5},{7,6},{8,15},{9,8},{10,9... | collective-permute-start | bytes 393224 | tf_op jit(solution)/shard_map/ppermute | solution.py:28
  42.6 9.2 %collective-permute-start.17 = (bf16[512,256]{1,0:T(8,128)(2,1)S(1)}, bf16[512,256]{1,0:T(8,128)(2,1)S(1)}, u32[]{:S(2)}, u32[]{:S(2)}) collective-permute-start(bf16[512,256]{1,0:T(8,128)(2,1)S(1)} %get-tuple-element.38), channel_id=1, source_target_pairs={{0,8},{8,0},{1,9},{9,1},{2,10},{10,2},{3,11},{11,3},{4,12},{12,4},... | collective-permute-start | bytes 786440 | tf_op jit(solution)/shard_map/ppermute | solution.py:28
  51.9 14.0 %collective-permute-start.19 = (bf16[1024,256]{1,0:T(8,128)(2,1)S(1)}, bf16[1024,256]{1,0:T(8,128)(2,1)S(1)}, u32[]{:S(2)}, u32[]{:S(2)}) collective-permute-start(bf16[1024,256]{1,0:T(8,128)(2,1)S(1)} %get-tuple-element.39.refs_1_), channel_id=1, source_target_pairs={{0,64},{64,0},{1,65},{65,1},{2,66},{66,2},{3,67},{67,3},{4,68},{68... | collective-permute-start | bytes 1572872 | tf_op jit(solution)/shard_map/ppermute | solution.py:28
  53.3 17.8 %collective-permute-start.21 = (bf16[1024,256]{1,0:T(8,128)(2,1)S(1)}, bf16[1024,256]{1,0:T(8,128)(2,1)S(1)}, u32[]{:S(2)}, u32[]{:S(2)}) collective-permute-start(bf16[1024,256]{1,0:T(8,128)(2,1)S(1)} %get-tuple-element.39.refs_1_), channel_id=1, source_target_pairs={{0,32},{32,0},{1,33},{33,1},{2,34},{34,2},{3,35},{35,3},{4,36},{36... | collective-permute-start | bytes 1572872 | tf_op jit(solution)/shard_map/ppermute | solution.py:28
  57.0 22.6 %collective-permute-start.20 = (bf16[1024,256]{1,0:T(8,128)(2,1)S(1)}, bf16[1024,256]{1,0:T(8,128)(2,1)S(1)}, u32[]{:S(2)}, u32[]{:S(2)}) collective-permute-start(bf16[1024,256]{1,0:T(8,128)(2,1)S(1)} %get-tuple-element.39.refs_1_), channel_id=1, source_target_pairs={{0,96},{32,64},{64,32},{96,0},{1,97},{33,65},{65,33},{97,1},{2,98}... | collective-permute-start | bytes 1572872 | tf_op jit(solution)/shard_map/ppermute | solution.py:28
  65.9 20.9 %all-to-all-start = ((bf16[16,128,128]{2,1,0:T(8,128)(2,1)}), bf16[16,128,128]{2,1,0:T(8,128)(2,1)S(1)}, u32[]{:S(2)}, u32[]{:S(2)}) async-start(bf16[16,128,128]{2,1,0:T(8,128)(2,1)} %column_parts.1), calls=%async_computation | async-start | bytes 1048576 | tf_op jit(solution)/shard_map/all_to_all | solution.py:302
  88.8 7.2 %collective-permute-start.25 = (bf16[512,128]{1,0:T(8,128)(2,1)S(1)}, bf16[512,128]{1,0:T(8,128)(2,1)S(1)}, u32[]{:S(2)}, u32[]{:S(2)}) collective-permute-start(bf16[512,128]{1,0:T(8,128)(2,1)S(1)} %get-tuple-element.50.refs_2_), channel_id=1, source_target_pairs={{0,7},{1,0},{2,1},{3,2},{4,3},{5,4},{6,5},{7,6},{8,15},{9,8},{10,9... | collective-permute-start | bytes 393224 | tf_op jit(solution)/shard_map/ppermute | solution.py:28
  92.7 27.4 %collective-permute-start.24 = (bf16[2048,128]{1,0:T(8,128)(2,1)S(1)}, bf16[2048,128]{1,0:T(8,128)(2,1)S(1)}, u32[]{:S(2)}, u32[]{:S(2)}) collective-permute-start(bf16[2048,128]{1,0:T(8,128)(2,1)S(1)} %bitcast.1), channel_id=1, source_target_pairs={{0,8},{8,0},{1,9},{9,1},{2,10},{10,2},{3,11},{11,3},{4,12},{12,4},... | collective-permute-start | bytes 1572872 | tf_op jit(solution)/shard_map/ppermute | solution.py:28
  101.8 7.5 %collective-permute-start.29 = (bf16[512,128]{1,0:T(8,128)(2,1)S(1)}, bf16[512,128]{1,0:T(8,128)(2,1)S(1)}, u32[]{:S(2)}, u32[]{:S(2)}) collective-permute-start(bf16[512,128]{1,0:T(8,128)(2,1)S(1)} %collective-permute-done.28.refs_6_), channel_id=1, source_target_pairs={{0,1},{1,2},{2,3},{3,4},{4,5},{5,6},{6,7},{7,0},{8,9},{9,10},{10,1... | collective-permute-start | bytes 393224 | tf_op jit(solution)/shard_map/ppermute | solution.py:28
  101.9 8.8 %collective-permute-start.33 = (bf16[512,128]{1,0:T(8,128)(2,1)S(1)}, bf16[512,128]{1,0:T(8,128)(2,1)S(1)}, u32[]{:S(2)}, u32[]{:S(2)}) collective-permute-start(bf16[512,128]{1,0:T(8,128)(2,1)S(1)} %collective-permute-done.31.refs_5_), channel_id=1, source_target_pairs={{0,7},{1,0},{2,1},{3,2},{4,3},{5,4},{6,5},{7,6},{8,15},{9,8},{10,9... | collective-permute-start | bytes 393224 | tf_op jit(solution)/shard_map/ppermute | solution.py:28
  105.1 7.5 %collective-permute-start.26 = (bf16[512,128]{1,0:T(8,128)(2,1)S(1)}, bf16[512,128]{1,0:T(8,128)(2,1)S(1)}, u32[]{:S(2)}, u32[]{:S(2)}) collective-permute-start(bf16[512,128]{1,0:T(8,128)(2,1)S(1)} %collective-permute-done.25.refs_4_), channel_id=1, source_target_pairs={{0,7},{1,0},{2,1},{3,2},{4,3},{5,4},{6,5},{7,6},{8,15},{9,8},{10,9... | collective-permute-start | bytes 393224 | tf_op jit(solution)/shard_map/ppermute | solution.py:28
  106.3 8.8 %collective-permute-start.34 = (bf16[512,128]{1,0:T(8,128)(2,1)S(1)}, bf16[512,128]{1,0:T(8,128)(2,1)S(1)}, u32[]{:S(2)}, u32[]{:S(2)}) collective-permute-start(bf16[512,128]{1,0:T(8,128)(2,1)S(1)} %collective-permute-done.32.refs_7_), channel_id=1, source_target_pairs={{0,1},{1,2},{2,3},{3,4},{4,5},{5,6},{6,7},{7,0},{8,9},{9,10},{10,1... | collective-permute-start | bytes 393224 | tf_op jit(solution)/shard_map/ppermute | solution.py:28
  109.4 7.4 %collective-permute-start.30 = (bf16[512,128]{1,0:T(8,128)(2,1)S(1)}, bf16[512,128]{1,0:T(8,128)(2,1)S(1)}, u32[]{:S(2)}, u32[]{:S(2)}) collective-permute-start(bf16[512,128]{1,0:T(8,128)(2,1)S(1)} %collective-permute-done.29.refs_10_), channel_id=1, source_target_pairs={{0,1},{1,2},{2,3},{3,4},{4,5},{5,6},{6,7},{7,0},{8,9},{9,10},{10,1... | collective-permute-start | bytes 393224 | tf_op jit(solution)/shard_map/ppermute | solution.py:28
  112.6 7.4 %collective-permute-start.27 = (bf16[512,128]{1,0:T(8,128)(2,1)S(1)}, bf16[512,128]{1,0:T(8,128)(2,1)S(1)}, u32[]{:S(2)}, u32[]{:S(2)}) collective-permute-start(bf16[512,128]{1,0:T(8,128)(2,1)S(1)} %collective-permute-done.26.refs_8_), channel_id=1, source_target_pairs={{0,7},{1,0},{2,1},{3,2},{4,3},{5,4},{6,5},{7,6},{8,15},{9,8},{10,9... | collective-permute-start | bytes 393224 | tf_op jit(solution)/shard_map/ppermute | solution.py:28
  (30 other events, 170.7 us)
where the time goes:
time: 131 us; the launch traced here: 129 us
  starting transfers between devices  62.2 us (47%)
  waiting for transfers between devices  36 us (27%)
  Pallas kernels  21.9 us (17%)
  local copies, waits for them, and re-layouts  8.73 us (7%)
    ppermute x40, starting transfers between devices, hop(): lax.ppermute(value, axes, [(number[c], number[tuple(target(*c))]) for c i...  57.1 us
    ppermute x40, waiting for transfers between devices, hop(): lax.ppermute(value, axes, [(number[c], number[tuple(target(*c))]) for c i...  34.3 us
    pallas_call x14, Pallas kernels, call(): pl.pallas_call(kernel, out_shape=outs, in_specs=[SMEM] * smem_count + [VM...  21.9 us
    unnamed x26, local copies, waits for them, and re-layouts  8.73 us
    all_to_all x1, starting transfers between devices, per_device(): lax.all_to_all(after(parts, own, from_y), HEAD, 0, 0)  5.16 us
  transfers between devices with their start and end apart: 41, of which 18 were waited for; matrix products, arithmetic and copies ran while one was open for 0% of the time, Pallas kernels for 15%

commit v1 on v0

--- a/solution.py
+++ b/solution.py
@@ -311,7 +311,7 @@
     )
     theirs = swap(other, "core")
     (own,) = attend(doc_lengths, [(unit, own, False)], [(6, from_yx)], "attend_far_own")
-    attended = combine(doc_lengths, after(own, w_cols), theirs, "combine")
+    attended = combine(doc_lengths, own, theirs, "combine")
 
     mine, theirs = gathered_product(
         attended,

time: 131 us -> 130 us (level)
  starting transfers between devices: 62.2 us -> 59.7 us
  waiting for transfers between devices: 36 us -> 37.6 us
    ppermute x40, waiting for transfers between devices: 34.3 us -> 37.6 us  [hop(): lax.ppermute(value, axes, [(number[c], number[tuple(target(*c))]) for c i...]
    ppermute x40, starting transfers between devices: 57.1 us -> 54.5 us  [hop(): lax.ppermute(value, axes, [(number[c], number[tuple(target(*c))]) for c i...]
    all_to_all x1, waiting for transfers between devices: 1.74 us -> 0.01 us  [per_device(): lax.all_to_all(after(parts, own, from_y), HEAD, 0, 0)]
    unnamed x26 -> x22, local copies, waits for them, and re-layouts: 8.73 us -> 7.77 us
  transfers between devices with their start and end apart: 41 -> 41, of which waited for: 18 -> 17; matrix products, arithmetic and copies ran while one was open for 0% -> 0% of each run, Pallas kernels for 15% -> 15%
where the time goes in v1:
time: 130 us; the launch traced here: 127 us
  starting transfers between devices  59.7 us (46%)
  waiting for transfers between devices  37.6 us (29%)
  Pallas kernels  21.9 us (17%)
  local copies, waits for them, and re-layouts  7.77 us (6%)
    ppermute x40, starting transfers between devices, hop(): lax.ppermute(value, axes, [(number[c], number[tuple(target(*c))]) for c i...  54.5 us
    ppermute x40, waiting for transfers between devices, hop(): lax.ppermute(value, axes, [(number[c], number[tuple(target(*c))]) for c i...  37.6 us
    pallas_call x14, Pallas kernels, call(): pl.pallas_call(kernel, out_shape=outs, in_specs=[SMEM] * smem_count + [VM...  21.9 us
    unnamed x22, local copies, waits for them, and re-layouts  7.77 us
    all_to_all x1, starting transfers between devices, per_device(): lax.all_to_all(after(parts, own, from_y), HEAD, 0, 0)  5.16 us
  transfers between devices with their start and end apart: 41, of which 17 were waited for; matrix products, arithmetic and copies ran while one was open for 0% of the time, Pallas kernels for 15%

profile of v1, /device:TPU:16, one launch (start us, length us, event | category | flops | bytes accessed | tf_op | source)
XLA Modules:
  0.0 127.1 jit_solution(2345083674096811041)
XLA Ops:
  4.5 3.9 %collective-permute-start.3 = (bf16[512,128]{1,0:T(8,128)(2,1)S(1)}, bf16[512,128]{1,0:T(8,128)(2,1)S(1)}, u32[]{:S(2)}, u32[]{:S(2)}) collective-permute-start(bf16[512,128]{1,0:T(8,128)(2,1)S(1)} %get-tuple-element.33.refs_4_), channel_id=1, source_target_pairs={{0,7},{1,0},{2,1},{3,2},{4,3},{5,4},{6,5},{7,6},{8,15},{9,8},{10,9... | collective-permute-start | bytes 393224 | tf_op jit(solution)/shard_map/ppermute | solution.py:28
  11.6 3.2 %collective-permute-start.4 = (bf16[512,128]{1,0:T(8,128)(2,1)S(1)}, bf16[512,128]{1,0:T(8,128)(2,1)S(1)}, u32[]{:S(2)}, u32[]{:S(2)}) collective-permute-start(bf16[512,128]{1,0:T(8,128)(2,1)S(1)} %collective-permute-done.3.refs_6_), channel_id=1, source_target_pairs={{0,7},{1,0},{2,1},{3,2},{4,3},{5,4},{6,5},{7,6},{8,15},{9,8},{10,9... | collective-permute-start | bytes 393224 | tf_op jit(solution)/shard_map/ppermute | solution.py:28
  17.9 2.0 %collective-permute-done.9.refs_7_ = bf16[512,128]{1,0:T(8,128)(2,1)S(1)} collective-permute-done((bf16[512,128]{1,0:T(8,128)(2,1)S(1)}, bf16[512,128]{1,0:T(8,128)(2,1)S(1)}, u32[]{:S(2)}, u32[]{:S(2)}) %collective-permute-start.9) | collective-permute-done | bytes 131104 | tf_op jit(solution)/shard_map/ppermute | solution.py:28
  19.8 3.1 %collective-permute-start.11 = (bf16[512,128]{1,0:T(8,128)(2,1)S(1)}, bf16[512,128]{1,0:T(8,128)(2,1)S(1)}, u32[]{:S(2)}, u32[]{:S(2)}) collective-permute-start(bf16[512,128]{1,0:T(8,128)(2,1)S(1)} %collective-permute-done.9.refs_7_), channel_id=1, source_target_pairs={{0,7},{1,0},{2,1},{3,2},{4,3},{5,4},{6,5},{7,6},{8,15},{9,8},{10,9... | collective-permute-start | bytes 393224 | tf_op jit(solution)/shard_map/ppermute | solution.py:28
  24.0 2.3 %collective-permute-done.8.refs_8_ = bf16[512,128]{1,0:T(8,128)(2,1)S(1)} collective-permute-done((bf16[512,128]{1,0:T(8,128)(2,1)S(1)}, bf16[512,128]{1,0:T(8,128)(2,1)S(1)}, u32[]{:S(2)}, u32[]{:S(2)}) %collective-permute-start.8) | collective-permute-done | bytes 131104 | tf_op jit(solution)/shard_map/ppermute | solution.py:28
  27.2 3.3 %collective-permute-start.13 = (bf16[512,128]{1,0:T(8,128)(2,1)S(1)}, bf16[512,128]{1,0:T(8,128)(2,1)S(1)}, u32[]{:S(2)}, u32[]{:S(2)}) collective-permute-start(bf16[512,128]{1,0:T(8,128)(2,1)S(1)} %collective-permute-done.11.refs_11_), channel_id=1, source_target_pairs={{0,7},{1,0},{2,1},{3,2},{4,3},{5,4},{6,5},{7,6},{8,15},{9,8},{10,9... | collective-permute-start | bytes 393224 | tf_op jit(solution)/shard_map/ppermute | solution.py:28
  31.8 2.6 %collective-permute-done.13.refs_7_ = bf16[512,128]{1,0:T(8,128)(2,1)S(1)} collective-permute-done((bf16[512,128]{1,0:T(8,128)(2,1)S(1)}, bf16[512,128]{1,0:T(8,128)(2,1)S(1)}, u32[]{:S(2)}, u32[]{:S(2)}) %collective-permute-start.13) | collective-permute-done | bytes 131104 | tf_op jit(solution)/shard_map/ppermute | solution.py:28
  34.4 3.7 %collective-permute-start.16 = (bf16[512,128]{1,0:T(8,128)(2,1)S(1)}, bf16[512,128]{1,0:T(8,128)(2,1)S(1)}, u32[]{:S(2)}, u32[]{:S(2)}) collective-permute-start(bf16[512,128]{1,0:T(8,128)(2,1)S(1)} %collective-permute-done.13.refs_7_), channel_id=1, source_target_pairs={{0,7},{1,0},{2,1},{3,2},{4,3},{5,4},{6,5},{7,6},{8,15},{9,8},{10,9... | collective-permute-start | bytes 393224 | tf_op jit(solution)/shard_map/ppermute | solution.py:28
  43.2 8.6 %collective-permute-done.17.t_ref = bf16[512,256]{1,0:T(8,128)(2,1)S(1)} collective-permute-done((bf16[512,256]{1,0:T(8,128)(2,1)S(1)}, bf16[512,256]{1,0:T(8,128)(2,1)S(1)}, u32[]{:S(2)}, u32[]{:S(2)}) %collective-permute-start.17) | collective-permute-done | bytes 262176 | tf_op jit(solution)/shard_map/ppermute | solution.py:28
  53.3 2.8 %collective-permute-start.21 = (bf16[1024,256]{1,0:T(8,128)(2,1)S(1)}, bf16[1024,256]{1,0:T(8,128)(2,1)S(1)}, u32[]{:S(2)}, u32[]{:S(2)}) collective-permute-start(bf16[1024,256]{1,0:T(8,128)(2,1)S(1)} %get-tuple-element.38.refs_1_), channel_id=1, source_target_pairs={{0,32},{32,0},{1,33},{33,1},{2,34},{34,2},{3,35},{35,3},{4,36},{36... | collective-permute-start | bytes 1572872 | tf_op jit(solution)/shard_map/ppermute | solution.py:28
  57.8 6.0 %attend_own.1 = (f32[1024,256]{1,0:T(8,128)S(1)}, f32[1024,256]{1,0:T(8,128)S(1)}) custom-call(s32[2]{0:T(128)S(1)} %copy-done.6, bf16[1024,256]{1,0:T(8,128)(2,1)S(1)} %get-tuple-element.38.refs_1_, bf16[1024,128]{1,0:T(8,128)(2,1)S(1)} %get-tuple-element.39.refs_2_.refs_3_, bf16[1024,128]{1,0:T(8,128)(2,1)S(1)} %collective-permute-done.18.refs_3_.refs_5_.refs_2_), custom_call_target="tpu_custom_call" | custom-call | flops 2147483648 | bytes 3145736 | tf_op jit(solution)/shard_map/attend_own/pallas_call | solution.py:46
  65.9 5.2 %all-to-all-start = ((bf16[16,128,128]{2,1,0:T(8,128)(2,1)}), bf16[16,128,128]{2,1,0:T(8,128)(2,1)S(1)}, u32[]{:S(2)}, u32[]{:S(2)}) async-start(bf16[16,128,128]{2,1,0:T(8,128)(2,1)} %column_parts.1), calls=%async_computation | async-start | bytes 1048576 | tf_op jit(solution)/shard_map/all_to_all | solution.py:302
  73.5 6.0 %attend_near.1 = (f32[1024,256]{1,0:T(8,128)S(1)}, f32[1024,256]{1,0:T(8,128)S(1)}) custom-call(s32[2]{0:T(128)S(1)} %copy-done.6, bf16[1024,256]{1,0:T(8,128)(2,1)S(1)} %collective-permute-done.19.refs_1_, bf16[1024,256]{1,0:T(8,128)(2,1)S(1)} %collective-permute-done.21.refs_2_, bf16[1024,128]{1,0:T(8,128)(2,1)S(1)} %get-tuple-element.39.refs_2_.refs_3_, ...), custom_call_target="tpu_custom_call" | custom-call | flops 4294967296 | bytes 5767176 | tf_op jit(solution)/shard_map/attend_near/pallas_call | solution.py:46
  79.6 2.2 %attend_far_other.1 = bf16[1024,256]{1,0:T(8,128)(2,1)S(1)} custom-call(s32[2]{0:T(128)S(1)} %copy-done.6, bf16[1024,256]{1,0:T(8,128)(2,1)S(1)} %collective-permute-done.20.refs_1_, bf16[1024,128]{1,0:T(8,128)(2,1)S(1)} %collective-permute-done.18.refs_3_.refs_5_.refs_2_, f32[1024,256]{1,0:T(8,128)S(1)} %get-tuple-element.44.refs_3_), custom_call_target="tpu_custom_call" | custom-call | flops 1073741824 | bytes 2359304 | tf_op jit(solution)/shard_map/attend_far_other/pallas_call | solution.py:46
  81.9 2.2 %attend_far_own.1.a_ref = f32[1024,256]{1,0:T(8,128)S(1)} custom-call(s32[2]{0:T(128)S(1)} %copy-done.6, bf16[1024,256]{1,0:T(8,128)(2,1)S(1)} %collective-permute-done.20.refs_1_, bf16[1024,128]{1,0:T(8,128)(2,1)S(1)} %get-tuple-element.39.refs_2_.refs_3_, f32[1024,256]{1,0:T(8,128)S(1)} %get-tuple-element.43.refs_3_), custom_call_target="tpu_custom_call" | custom-call | flops 1073741824 | bytes 2883592 | tf_op jit(solution)/shard_map/attend_far_own/pallas_call | solution.py:46
  84.9 2.0 %collective-permute-start.23 = (bf16[512,128]{1,0:T(8,128)(2,1)S(1)}, bf16[512,128]{1,0:T(8,128)(2,1)S(1)}, u32[]{:S(2)}, u32[]{:S(2)}) collective-permute-start(bf16[512,128]{1,0:T(8,128)(2,1)S(1)} %get-tuple-element.45), channel_id=1, source_target_pairs={{0,8},{8,0},{1,9},{9,1},{2,10},{10,2},{3,11},{11,3},{4,12},{12,4},... | collective-permute-start | bytes 393224 | tf_op jit(solution)/shard_map/ppermute | solution.py:28
  86.9 2.7 %collective-permute-start.25 = (bf16[512,128]{1,0:T(8,128)(2,1)S(1)}, bf16[512,128]{1,0:T(8,128)(2,1)S(1)}, u32[]{:S(2)}, u32[]{:S(2)}) collective-permute-start(bf16[512,128]{1,0:T(8,128)(2,1)S(1)} %get-tuple-element.48.refs_2_), channel_id=1, source_target_pairs={{0,7},{1,0},{2,1},{3,2},{4,3},{5,4},{6,5},{7,6},{8,15},{9,8},{10,9... | collective-permute-start | bytes 393224 | tf_op jit(solution)/shard_map/ppermute | solution.py:28
  94.2 2.1 %collective-permute-start.31 = (bf16[512,128]{1,0:T(8,128)(2,1)S(1)}, bf16[512,128]{1,0:T(8,128)(2,1)S(1)}, u32[]{:S(2)}, u32[]{:S(2)}) collective-permute-start(bf16[512,128]{1,0:T(8,128)(2,1)S(1)} %collective-permute-done.23.refs_3_), channel_id=1, source_target_pairs={{0,7},{1,0},{2,1},{3,2},{4,3},{5,4},{6,5},{7,6},{8,15},{9,8},{10,9... | collective-permute-start | bytes 393224 | tf_op jit(solution)/shard_map/ppermute | solution.py:28
  96.4 2.6 %collective-permute-done.28.refs_6_ = bf16[512,128]{1,0:T(8,128)(2,1)S(1)} collective-permute-done((bf16[512,128]{1,0:T(8,128)(2,1)S(1)}, bf16[512,128]{1,0:T(8,128)(2,1)S(1)}, u32[]{:S(2)}, u32[]{:S(2)}) %collective-permute-start.28) | collective-permute-done | bytes 131104 | tf_op jit(solution)/shard_map/ppermute | solution.py:28
  107.2 3.2 %collective-permute-start.35 = (bf16[512,128]{1,0:T(8,128)(2,1)S(1)}, bf16[512,128]{1,0:T(8,128)(2,1)S(1)}, u32[]{:S(2)}, u32[]{:S(2)}) collective-permute-start(bf16[512,128]{1,0:T(8,128)(2,1)S(1)} %collective-permute-done.33.refs_9_), channel_id=1, source_target_pairs={{0,7},{1,0},{2,1},{3,2},{4,3},{5,4},{6,5},{7,6},{8,15},{9,8},{10,9... | collective-permute-start | bytes 393224 | tf_op jit(solution)/shard_map/ppermute | solution.py:28
  112.5 2.3 %collective-permute-done.30.refs_5_ = bf16[512,128]{1,0:T(8,128)(2,1)S(1)} collective-permute-done((bf16[512,128]{1,0:T(8,128)(2,1)S(1)}, bf16[512,128]{1,0:T(8,128)(2,1)S(1)}, u32[]{:S(2)}, u32[]{:S(2)}) %collective-permute-start.30) | collective-permute-done | bytes 131104 | tf_op jit(solution)/shard_map/ppermute | solution.py:28
  114.8 3.2 %collective-permute-start.38 = (bf16[512,128]{1,0:T(8,128)(2,1)S(1)}, bf16[512,128]{1,0:T(8,128)(2,1)S(1)}, u32[]{:S(2)}, u32[]{:S(2)}) collective-permute-start(bf16[512,128]{1,0:T(8,128)(2,1)S(1)} %collective-permute-done.35.refs_4_), channel_id=1, source_target_pairs={{0,7},{1,0},{2,1},{3,2},{4,3},{5,4},{6,5},{7,6},{8,15},{9,8},{10,9... | collective-permute-start | bytes 393224 | tf_op jit(solution)/shard_map/ppermute | solution.py:28
  118.5 2.4 %collective-permute-done.37.refs_7_ = bf16[512,128]{1,0:T(8,128)(2,1)S(1)} collective-permute-done((bf16[512,128]{1,0:T(8,128)(2,1)S(1)}, bf16[512,128]{1,0:T(8,128)(2,1)S(1)}, u32[]{:S(2)}, u32[]{:S(2)}) %collective-permute-start.37) | collective-permute-done | bytes 131104 | tf_op jit(solution)/shard_map/ppermute | solution.py:28
  121.8 4.6 %collective-permute-done.39.t_ref = bf16[512,128]{1,0:T(8,128)(2,1)S(1)} collective-permute-done((bf16[512,128]{1,0:T(8,128)(2,1)S(1)}, bf16[512,128]{1,0:T(8,128)(2,1)S(1)}, u32[]{:S(2)}, u32[]{:S(2)}) %collective-permute-start.39) | collective-permute-done | bytes 131104 | tf_op jit(solution)/shard_map/ppermute | solution.py:28
  (94 shorter events, 44.7 us)
Async XLA Ops:
  1.0 7.4 %collective-permute-start = (bf16[512,128]{1,0:T(8,128)(2,1)S(1)}, bf16[512,128]{1,0:T(8,128)(2,1)S(1)}, u32[]{:S(2)}, u32[]{:S(2)}) collective-permute-start(bf16[512,128]{1,0:T(8,128)(2,1)S(1)} %get-tuple-element.29), channel_id=1, source_target_pairs={{0,8},{8,0},{1,9},{9,1},{2,10},{10,2},{3,11},{11,3},{4,12},{12,4},... | collective-permute-start | bytes 393224 | tf_op jit(solution)/shard_map/ppermute | solution.py:28
  2.6 9.1 %collective-permute-start.6 = (bf16[512,128]{1,0:T(8,128)(2,1)S(1)}, bf16[512,128]{1,0:T(8,128)(2,1)S(1)}, u32[]{:S(2)}, u32[]{:S(2)}) collective-permute-start(bf16[512,128]{1,0:T(8,128)(2,1)S(1)} %get-tuple-element.33.refs_4_), channel_id=1, source_target_pairs={{0,1},{1,2},{2,3},{3,4},{4,5},{5,6},{6,7},{7,0},{8,9},{9,10},{10,1... | collective-permute-start | bytes 393224 | tf_op jit(solution)/shard_map/ppermute | solution.py:28
  4.5 7.2 %collective-permute-start.3 = (bf16[512,128]{1,0:T(8,128)(2,1)S(1)}, bf16[512,128]{1,0:T(8,128)(2,1)S(1)}, u32[]{:S(2)}, u32[]{:S(2)}) collective-permute-start(bf16[512,128]{1,0:T(8,128)(2,1)S(1)} %get-tuple-element.33.refs_4_), channel_id=1, source_target_pairs={{0,7},{1,0},{2,1},{3,2},{4,3},{5,4},{6,5},{7,6},{8,15},{9,8},{10,9... | collective-permute-start | bytes 393224 | tf_op jit(solution)/shard_map/ppermute | solution.py:28
  8.4 29.6 %collective-permute-start.1 = (bf16[2048,128]{1,0:T(8,128)(2,1)}, bf16[2048,128]{1,0:T(8,128)(2,1)S(1)}, u32[]{:S(2)}, u32[]{:S(2)}) collective-permute-start(bf16[2048,128]{1,0:T(8,128)(2,1)} %refs_1_.3), channel_id=1, source_target_pairs={{0,8},{8,0},{1,9},{9,1},{2,10},{10,2},{3,11},{11,3},{4,12},{12,4},... | collective-permute-start | bytes 1572872 | tf_op jit(solution)/shard_map/ppermute | solution.py:28
  9.0 29.1 %collective-permute-start.2 = (bf16[2048,128]{1,0:T(8,128)(2,1)}, bf16[2048,128]{1,0:T(8,128)(2,1)S(1)}, u32[]{:S(2)}, u32[]{:S(2)}) collective-permute-start(bf16[2048,128]{1,0:T(8,128)(2,1)} %refs_2_.1), channel_id=1, source_target_pairs={{0,8},{8,0},{1,9},{9,1},{2,10},{10,2},{3,11},{11,3},{4,12},{12,4},... | collective-permute-start | bytes 1572872 | tf_op jit(solution)/shard_map/ppermute | solution.py:28
  17.9 8.4 %collective-permute-start.8 = (bf16[512,128]{1,0:T(8,128)(2,1)S(1)}, bf16[512,128]{1,0:T(8,128)(2,1)S(1)}, u32[]{:S(2)}, u32[]{:S(2)}) collective-permute-start(bf16[512,128]{1,0:T(8,128)(2,1)S(1)} %collective-permute-done.7.refs_12_), channel_id=1, source_target_pairs={{0,1},{1,2},{2,3},{3,4},{4,5},{5,6},{6,7},{7,0},{8,9},{9,10},{10,1... | collective-permute-start | bytes 393224 | tf_op jit(solution)/shard_map/ppermute | solution.py:28
  19.8 7.4 %collective-permute-start.11 = (bf16[512,128]{1,0:T(8,128)(2,1)S(1)}, bf16[512,128]{1,0:T(8,128)(2,1)S(1)}, u32[]{:S(2)}, u32[]{:S(2)}) collective-permute-start(bf16[512,128]{1,0:T(8,128)(2,1)S(1)} %collective-permute-done.9.refs_7_), channel_id=1, source_target_pairs={{0,7},{1,0},{2,1},{3,2},{4,3},{5,4},{6,5},{7,6},{8,15},{9,8},{10,9... | collective-permute-start | bytes 393224 | tf_op jit(solution)/shard_map/ppermute | solution.py:28
  27.2 7.2 %collective-permute-start.13 = (bf16[512,128]{1,0:T(8,128)(2,1)S(1)}, bf16[512,128]{1,0:T(8,128)(2,1)S(1)}, u32[]{:S(2)}, u32[]{:S(2)}) collective-permute-start(bf16[512,128]{1,0:T(8,128)(2,1)S(1)} %collective-permute-done.11.refs_11_), channel_id=1, source_target_pairs={{0,7},{1,0},{2,1},{3,2},{4,3},{5,4},{6,5},{7,6},{8,15},{9,8},{10,9... | collective-permute-start | bytes 393224 | tf_op jit(solution)/shard_map/ppermute | solution.py:28
  30.6 10.5 %collective-permute-start.14 = (bf16[512,128]{1,0:T(8,128)(2,1)S(1)}, bf16[512,128]{1,0:T(8,128)(2,1)S(1)}, u32[]{:S(2)}, u32[]{:S(2)}) collective-permute-start(bf16[512,128]{1,0:T(8,128)(2,1)S(1)} %collective-permute-done.12.refs_13_), channel_id=1, source_target_pairs={{0,1},{1,2},{2,3},{3,4},{4,5},{5,6},{6,7},{7,0},{8,9},{9,10},{10,1... | collective-permute-start | bytes 393224 | tf_op jit(solution)/shard_map/ppermute | solution.py:28
  31.8 9.2 %collective-permute-start.15 = (bf16[512,128]{1,0:T(8,128)(2,1)S(1)}, bf16[512,128]{1,0:T(8,128)(2,1)S(1)}, u32[]{:S(2)}, u32[]{:S(2)}) collective-permute-start(bf16[512,128]{1,0:T(8,128)(2,1)S(1)} %collective-permute-done.8.refs_8_), channel_id=1, source_target_pairs={{0,1},{1,2},{2,3},{3,4},{4,5},{5,6},{6,7},{7,0},{8,9},{9,10},{10,1... | collective-permute-start | bytes 393224 | tf_op jit(solution)/shard_map/ppermute | solution.py:28
  34.4 6.7 %collective-permute-start.16 = (bf16[512,128]{1,0:T(8,128)(2,1)S(1)}, bf16[512,128]{1,0:T(8,128)(2,1)S(1)}, u32[]{:S(2)}, u32[]{:S(2)}) collective-permute-start(bf16[512,128]{1,0:T(8,128)(2,1)S(1)} %collective-permute-done.13.refs_7_), channel_id=1, source_target_pairs={{0,7},{1,0},{2,1},{3,2},{4,3},{5,4},{6,5},{7,6},{8,15},{9,8},{10,9... | collective-permute-start | bytes 393224 | tf_op jit(solution)/shard_map/ppermute | solution.py:28
  42.6 9.2 %collective-permute-start.17 = (bf16[512,256]{1,0:T(8,128)(2,1)S(1)}, bf16[512,256]{1,0:T(8,128)(2,1)S(1)}, u32[]{:S(2)}, u32[]{:S(2)}) collective-permute-start(bf16[512,256]{1,0:T(8,128)(2,1)S(1)} %get-tuple-element.37), channel_id=1, source_target_pairs={{0,8},{8,0},{1,9},{9,1},{2,10},{10,2},{3,11},{11,3},{4,12},{12,4},... | collective-permute-start | bytes 786440 | tf_op jit(solution)/shard_map/ppermute | solution.py:28
  51.9 14.0 %collective-permute-start.19 = (bf16[1024,256]{1,0:T(8,128)(2,1)S(1)}, bf16[1024,256]{1,0:T(8,128)(2,1)S(1)}, u32[]{:S(2)}, u32[]{:S(2)}) collective-permute-start(bf16[1024,256]{1,0:T(8,128)(2,1)S(1)} %get-tuple-element.38.refs_1_), channel_id=1, source_target_pairs={{0,64},{64,0},{1,65},{65,1},{2,66},{66,2},{3,67},{67,3},{4,68},{68... | collective-permute-start | bytes 1572872 | tf_op jit(solution)/shard_map/ppermute | solution.py:28
  53.3 17.7 %collective-permute-start.21 = (bf16[1024,256]{1,0:T(8,128)(2,1)S(1)}, bf16[1024,256]{1,0:T(8,128)(2,1)S(1)}, u32[]{:S(2)}, u32[]{:S(2)}) collective-permute-start(bf16[1024,256]{1,0:T(8,128)(2,1)S(1)} %get-tuple-element.38.refs_1_), channel_id=1, source_target_pairs={{0,32},{32,0},{1,33},{33,1},{2,34},{34,2},{3,35},{35,3},{4,36},{36... | collective-permute-start | bytes 1572872 | tf_op jit(solution)/shard_map/ppermute | solution.py:28
  57.0 22.6 %collective-permute-start.20 = (bf16[1024,256]{1,0:T(8,128)(2,1)S(1)}, bf16[1024,256]{1,0:T(8,128)(2,1)S(1)}, u32[]{:S(2)}, u32[]{:S(2)}) collective-permute-start(bf16[1024,256]{1,0:T(8,128)(2,1)S(1)} %get-tuple-element.38.refs_1_), channel_id=1, source_target_pairs={{0,96},{32,64},{64,32},{96,0},{1,97},{33,65},{65,33},{97,1},{2,98}... | collective-permute-start | bytes 1572872 | tf_op jit(solution)/shard_map/ppermute | solution.py:28
  65.9 25.2 %all-to-all-start = ((bf16[16,128,128]{2,1,0:T(8,128)(2,1)}), bf16[16,128,128]{2,1,0:T(8,128)(2,1)S(1)}, u32[]{:S(2)}, u32[]{:S(2)}) async-start(bf16[16,128,128]{2,1,0:T(8,128)(2,1)} %column_parts.1), calls=%async_computation | async-start | bytes 1048576 | tf_op jit(solution)/shard_map/all_to_all | solution.py:302
  86.9 7.4 %collective-permute-start.25 = (bf16[512,128]{1,0:T(8,128)(2,1)S(1)}, bf16[512,128]{1,0:T(8,128)(2,1)S(1)}, u32[]{:S(2)}, u32[]{:S(2)}) collective-permute-start(bf16[512,128]{1,0:T(8,128)(2,1)S(1)} %get-tuple-element.48.refs_2_), channel_id=1, source_target_pairs={{0,7},{1,0},{2,1},{3,2},{4,3},{5,4},{6,5},{7,6},{8,15},{9,8},{10,9... | collective-permute-start | bytes 393224 | tf_op jit(solution)/shard_map/ppermute | solution.py:28
  91.0 27.0 %collective-permute-start.24 = (bf16[2048,128]{1,0:T(8,128)(2,1)S(1)}, bf16[2048,128]{1,0:T(8,128)(2,1)S(1)}, u32[]{:S(2)}, u32[]{:S(2)}) collective-permute-start(bf16[2048,128]{1,0:T(8,128)(2,1)S(1)} %bitcast.1), channel_id=1, source_target_pairs={{0,8},{8,0},{1,9},{9,1},{2,10},{10,2},{3,11},{11,3},{4,12},{12,4},... | collective-permute-start | bytes 1572872 | tf_op jit(solution)/shard_map/ppermute | solution.py:28
  99.2 8.0 %collective-permute-start.29 = (bf16[512,128]{1,0:T(8,128)(2,1)S(1)}, bf16[512,128]{1,0:T(8,128)(2,1)S(1)}, u32[]{:S(2)}, u32[]{:S(2)}) collective-permute-start(bf16[512,128]{1,0:T(8,128)(2,1)S(1)} %collective-permute-done.28.refs_6_), channel_id=1, source_target_pairs={{0,1},{1,2},{2,3},{3,4},{4,5},{5,6},{6,7},{7,0},{8,9},{9,10},{10,1... | collective-permute-start | bytes 393224 | tf_op jit(solution)/shard_map/ppermute | solution.py:28
  102.6 7.9 %collective-permute-start.26 = (bf16[512,128]{1,0:T(8,128)(2,1)S(1)}, bf16[512,128]{1,0:T(8,128)(2,1)S(1)}, u32[]{:S(2)}, u32[]{:S(2)}) collective-permute-start(bf16[512,128]{1,0:T(8,128)(2,1)S(1)} %collective-permute-done.25.refs_4_), channel_id=1, source_target_pairs={{0,7},{1,0},{2,1},{3,2},{4,3},{5,4},{6,5},{7,6},{8,15},{9,8},{10,9... | collective-permute-start | bytes 393224 | tf_op jit(solution)/shard_map/ppermute | solution.py:28
  107.2 7.6 %collective-permute-start.30 = (bf16[512,128]{1,0:T(8,128)(2,1)S(1)}, bf16[512,128]{1,0:T(8,128)(2,1)S(1)}, u32[]{:S(2)}, u32[]{:S(2)}) collective-permute-start(bf16[512,128]{1,0:T(8,128)(2,1)S(1)} %collective-permute-done.29.refs_10_), channel_id=1, source_target_pairs={{0,1},{1,2},{2,3},{3,4},{4,5},{5,6},{6,7},{7,0},{8,9},{9,10},{10,1... | collective-permute-start | bytes 393224 | tf_op jit(solution)/shard_map/ppermute | solution.py:28
  107.2 7.6 %collective-permute-start.35 = (bf16[512,128]{1,0:T(8,128)(2,1)S(1)}, bf16[512,128]{1,0:T(8,128)(2,1)S(1)}, u32[]{:S(2)}, u32[]{:S(2)}) collective-permute-start(bf16[512,128]{1,0:T(8,128)(2,1)S(1)} %collective-permute-done.33.refs_9_), channel_id=1, source_target_pairs={{0,7},{1,0},{2,1},{3,2},{4,3},{5,4},{6,5},{7,6},{8,15},{9,8},{10,9... | collective-permute-start | bytes 393224 | tf_op jit(solution)/shard_map/ppermute | solution.py:28
  110.4 7.6 %collective-permute-start.27 = (bf16[512,128]{1,0:T(8,128)(2,1)S(1)}, bf16[512,128]{1,0:T(8,128)(2,1)S(1)}, u32[]{:S(2)}, u32[]{:S(2)}) collective-permute-start(bf16[512,128]{1,0:T(8,128)(2,1)S(1)} %collective-permute-done.26.refs_8_), channel_id=1, source_target_pairs={{0,7},{1,0},{2,1},{3,2},{4,3},{5,4},{6,5},{7,6},{8,15},{9,8},{10,9... | collective-permute-start | bytes 393224 | tf_op jit(solution)/shard_map/ppermute | solution.py:28
  111.4 7.1 %collective-permute-start.36 = (bf16[512,128]{1,0:T(8,128)(2,1)S(1)}, bf16[512,128]{1,0:T(8,128)(2,1)S(1)}, u32[]{:S(2)}, u32[]{:S(2)}) collective-permute-start(bf16[512,128]{1,0:T(8,128)(2,1)S(1)} %collective-permute-done.34.refs_11_), channel_id=1, source_target_pairs={{0,1},{1,2},{2,3},{3,4},{4,5},{5,6},{6,7},{7,0},{8,9},{9,10},{10,1... | collective-permute-start | bytes 393224 | tf_op jit(solution)/shard_map/ppermute | solution.py:28
  (28 other events, 156.7 us)
